TPU v7x, 128 devices: a whole 4x4x4 slice. The times are simulated.
128 devices in a mesh: frame: 8 (over z_lo, y), pixel: 16 (over x, z_hi, core).
Axes of the slice: x: 4, y: 4, z: 4 (z_hi: 2, z_lo: 2; z = z_hi * 2 + z_lo), core: 2. Of those that a mesh axis runs over, the one named last changes fastest.
Arguments:
- intensity: float32 [4096, 16384], P('frame', 'pixel'), may hold values from 0.2 to 180, as said below
- cycle_label: int32 [16384], P('pixel'), may hold values from 0 to 15, as said below
Outputs:
- correlation: float32 [16, 4096, 4096], P('pixel', 'frame')
Inputs may be any that keep to these rules, and one draw needn't show every extreme that they name: `cycle_label`: labels never fall along the pixels; for r >= 1 the first pixel of cycle r lies before position r * 1024 and at most 512 positions before it; every cycle holds at least one pixel. `intensity`: positive intensities.
All inputs are finite; a program needn't handle non-finite values.
Results may differ from a plain program's by a relative error of at most 0.0003.
Values sent between devices are 32-bit elements; how exact they have to be, the bound alone decides.
A program may use at most 128 MiB of HBM per device.

v0:
```python
import math

import jax
import jax.numpy as jnp
from jax import lax
from jax.sharding import PartitionSpec as P

CYCLES = 16


def shifted(block, axis, distance):
    devices = range(lax.axis_size(axis))
    route = [(i - distance, i) for i in devices if i - distance in devices]
    return lax.ppermute(block, axis, route)


def cycle_panels(frame_rows, columns, labels, cycle_base, slot_count):
    pixel_count = labels.shape[0]
    block_width = math.gcd(pixel_count, 512)

    def add_block(block_index, panels):
        block_start = block_index * block_width
        row_part = lax.dynamic_slice_in_dim(frame_rows, block_start, block_width, 1)
        column_part = lax.dynamic_slice_in_dim(columns, block_start, block_width, 1)
        label_part = lax.dynamic_slice_in_dim(labels, block_start, block_width, 0)

        def add_cycle(cycle_id, panels_now):
            masked = row_part * (label_part == cycle_id).astype(row_part.dtype)[None, :]
            product = lax.dot_general(
                masked, column_part, (((1,), (1,)), ((), ())), precision=lax.Precision.HIGHEST
            )
            return panels_now.at[cycle_id - cycle_base].add(product)

        return lax.fori_loop(label_part[0], label_part[block_width - 1] + 1, add_cycle, panels)

    zero_panels = jnp.zeros((slot_count, frame_rows.shape[0], columns.shape[0]), jnp.float32)
    return lax.fori_loop(0, pixel_count // block_width, add_block, zero_panels)


def shards(intensity, cycle_label):
    own_cycles = CYCLES // lax.axis_size("pixel")
    slot_count = 2 * own_cycles
    cycle_base = lax.axis_index("pixel") * own_cycles
    slot_ids = cycle_base + jnp.arange(slot_count, dtype=jnp.int32)
    onehot_slot = (cycle_label[:, None] == slot_ids[None, :]).astype(jnp.float32)
    slot_sums = jnp.dot(intensity, onehot_slot, precision=lax.Precision.HIGHEST)
    slot_counts = jnp.sum(onehot_slot, axis=0)
    gathered = lax.all_gather(intensity, "frame", axis=0, tiled=True)
    panels = cycle_panels(intensity, gathered, cycle_label, cycle_base, slot_count)
    from_left, sums_left, counts_left = shifted(
        (panels[own_cycles:], slot_sums[:, own_cycles:], slot_counts[own_cycles:]), "pixel", 1
    )
    owned_maps = panels[:own_cycles] + from_left
    row_totals = slot_sums[:, :own_cycles] + sums_left
    own_counts = slot_counts[:own_cycles] + counts_left
    frame_sums = lax.all_gather(row_totals, "frame", axis=0, tiled=True)
    row_sums = row_totals.T
    column_sums = frame_sums.T
    return owned_maps * own_counts[:, None, None] / (row_sums[:, :, None] * column_sums[:, None, :])


def solution(mesh):
    in_specs = (P("frame", "pixel"), P("pixel"))
    out_specs = P("pixel", "frame", None)
    return jax.shard_map(shards, mesh=mesh, in_specs=in_specs, out_specs=out_specs, check_vma=False)
```

profile of v0, /device:TPU:7, one launch (start us, length us, event | category | flops | bytes accessed | tf_op | source)
XLA Modules:
  0.0 414.8 jit_solution(14316529880174144702)
XLA Ops:
  6.5 0.0 all-gather.2.cloned.1.call-start
  6.5 0.7 all-gather.2.cloned.1.call-update
  7.3 0.0 copy-start.1
  7.3 0.0 copy-start.2
  7.3 0.0 copy-start.3
  7.3 174.7 %all-gather.2.cloned.1.call-done = f32[4096,1024]{1,0:T(8,128)} async-done(((f32[512,1024]{1,0:T(8,128)}), f32[4096,1024]{1,0:T(8,128)}) %all-gather.2.cloned.1.call-update) | async-done | bytes 16777232 | tf_op jit(solution)/shard_map/all_gather | solution.py:48
  182.0 7.8 %broadcast_in_dim.2 = f32[2,512,4096]{2,1,0:T(8,128)} broadcast(f32[]{:T(128)} %constant.66.clone.1), dimensions={} | broadcast | bytes 16777220 | tf_op jit(solution)/shard_map/broadcast_in_dim | solution.py:36
  189.8 0.0 copy-done.1
  189.8 0.0 copy-done.2
  189.8 0.0 copy-done.3
  189.8 86.3 %while.35 = (s32[]{:T(128)}, f32[2,512,4096]{2,1,0:T(8,128)}, s32[1024]{0:T(1024)S(1)}, f32[512,1024]{1,0:T(8,128)S(1)}, f32[4096,1024]{1,0:T(8,128)}, /*index=5...) while((s32[]{:T(128)}, f32[2,512,4096]{2,1,0:T(8,128)}, ...), condition=%wide.region_4.5_spmd, body=%wide.region_0.4_spmd.sunk | while | flops 12889359360 | bytes 45100576 | solution.py:37
  189.8 0.1 dynamic_slice.28
  189.9 0.6 fusion.15
  191.1 0.1 constant_dynamic-slice_fusion.4
  191.2 7.8 %constant_dynamic-slice_fusion.5 = f32[4096,512]{1,0:T(8,128)} fusion(f32[4096,1024]{1,0:T(8,128)} %get-tuple-element.370, s32[]{:T(128)S(6)} %select_n.16), kind=kLoop, calls=%fused_computation.6.clone.1 | loop fusion | bytes 16777220 | tf_op jit(solution)/shard_map/while/body/eval_jaxpr/dynamic_slice | solution.py:24
  199.0 22.8 %while.36 = (s32[]{:T(128)}, f32[2,512,4096]{2,1,0:T(8,128)}, s32[]{:T(128)}, s32[]{:T(128)}, s32[512]{0:T(512)S(1)}, /*index=5*/f32[512,512]{1,0:T(8,128)S(1)},...) while((s32[]{:T(128)}, f32[2,512,4096]{2,1,0:T(8,128)}, ...), condition=%wide.region_3.3_spmd, body=%wide.region_1.2_spmd.sunk | while | flops 12889359360 | bytes 26221764 | solution.py:34
  200.2 0.7 and_reduce_fusion.2
  200.9 19.8 %fusion.18 = f32[2,512,4096]{2,1,0:T(8,128)} fusion(f32[2,512,4096]{2,1,0:T(8,128)} %get-tuple-element.311, s32[]{:T(128)} %select_n.17, f32[4096,512]{1,0:T(8,128)} %get-tuple-element.328, pred[]{:T(512)} %and_reduce_fusion.2, f32[512,512]{1,0:T(8,128)S(1)} %get-tuple-element.327, f32[512]{0:T(512)S(1)} %compare_convert_fusion.3), kind=kOutput, calls=%fused_computation.1.clone.1 | convolution fusion | flops 12889358336 | bytes 26217472 | tf_op jit(solution)/shard_map/while/body/eval_jaxpr/while/body/dot_general | solution.py:29
  221.8 0.1 dynamic_slice.28
  221.9 0.6 fusion.15
  223.2 0.1 constant_dynamic-slice_fusion.4
  223.3 7.8 %constant_dynamic-slice_fusion.5 = f32[4096,512]{1,0:T(8,128)} fusion(f32[4096,1024]{1,0:T(8,128)} %get-tuple-element.370, s32[]{:T(128)S(6)} %select_n.16), kind=kLoop, calls=%fused_computation.6.clone.1 | loop fusion | bytes 16777220 | tf_op jit(solution)/shard_map/while/body/eval_jaxpr/dynamic_slice | solution.py:24
  231.0 45.1 %while.36 = (s32[]{:T(128)}, f32[2,512,4096]{2,1,0:T(8,128)}, s32[]{:T(128)}, s32[]{:T(128)}, s32[512]{0:T(512)S(1)}, /*index=5*/f32[512,512]{1,0:T(8,128)S(1)},...) while((s32[]{:T(128)}, f32[2,512,4096]{2,1,0:T(8,128)}, ...), condition=%wide.region_3.3_spmd, body=%wide.region_1.2_spmd.sunk | while | flops 12889359360 | bytes 26221764 | solution.py:34
  232.2 0.7 and_reduce_fusion.2
  232.9 19.8 %fusion.18 = f32[2,512,4096]{2,1,0:T(8,128)} fusion(f32[2,512,4096]{2,1,0:T(8,128)} %get-tuple-element.311, s32[]{:T(128)} %select_n.17, f32[4096,512]{1,0:T(8,128)} %get-tuple-element.328, pred[]{:T(512)} %and_reduce_fusion.2, f32[512,512]{1,0:T(8,128)S(1)} %get-tuple-element.327, f32[512]{0:T(512)S(1)} %compare_convert_fusion.3), kind=kOutput, calls=%fused_computation.1.clone.1 | convolution fusion | flops 12889358336 | bytes 26217472 | tf_op jit(solution)/shard_map/while/body/eval_jaxpr/while/body/dot_general | solution.py:29
  254.4 0.7 and_reduce_fusion.2
  255.1 19.9 %fusion.18 = f32[2,512,4096]{2,1,0:T(8,128)} fusion(f32[2,512,4096]{2,1,0:T(8,128)} %get-tuple-element.311, s32[]{:T(128)} %select_n.17, f32[4096,512]{1,0:T(8,128)} %get-tuple-element.328, pred[]{:T(512)} %and_reduce_fusion.2, f32[512,512]{1,0:T(8,128)S(1)} %get-tuple-element.327, f32[512]{0:T(512)S(1)} %compare_convert_fusion.3), kind=kOutput, calls=%fused_computation.1.clone.1 | convolution fusion | flops 12889358336 | bytes 26217472 | tf_op jit(solution)/shard_map/while/body/eval_jaxpr/while/body/dot_general | solution.py:29
  276.1 0.0 copy-start
  276.1 8.8 %slice.52 = f32[1,512,4096]{2,1,0:T(8,128)} slice(f32[2,512,4096]{2,1,0:T(8,128)} %get-tuple-element.389), slice={[1:2], [0:512], [0:4096]} | slice | bytes 16777216 | tf_op jit(solution)/shard_map/slice | solution.py:51
  284.9 5.3 %collective-permute-start = (f32[1,512,4096]{2,1,0:T(8,128)}, f32[1,512,4096]{2,1,0:T(8,128)}, u32[]{:S(2)}, u32[]{:S(2)}) collective-permute-start(f32[1,512,4096]{2,1,0:T(8,128)} %slice.52), channel_id=1, source_target_pairs={{0,1},{1,2},{2,3},{3,4},{4,5},{5,6},{6,7},{7,8},{8,9},{9,10},{10,1... | collective-permute-start | bytes 25165832 | tf_op jit(solution)/shard_map/ppermute | solution.py:14
  290.2 1.1 convolution_bitcast_fusion
  291.3 1.9 collective-permute-start.2
  293.2 0.2 fusion.4
  293.4 0.6 fusion.8
  294.0 1.9 collective-permute-start.1
  296.0 84.9 %collective-permute-done.1 = f32[1]{0:T(128)} collective-permute-done((f32[1]{0:T(128)}, f32[1]{0:T(128)}, u32[]{:S(2)}, u32[]{:S(2)}) %collective-permute-start.1) | collective-permute-done | bytes 36 | tf_op jit(solution)/shard_map/ppermute | solution.py:14
  382.2 0.0 collective-permute-done.2
  382.2 19.1 %all_gather.7 = f32[4096,1]{0,1:T(1,128)S(1)} all-gather(f32[512,1]{0,1:T(1,128)S(1)} %slice_add_fusion), channel_id=1, replica_groups=mesh['frame'=8,'pixel'=16] {'frame'}, dimensions={0}, use_global_device_ids=true | all-gather | bytes 18432 | tf_op jit(solution)/shard_map/all_gather | solution.py:56
  401.3 0.0 collective-permute-done
  401.3 0.0 copy-done
  401.3 6.6 %multiply_divide_fusion = f32[1,512,4096]{2,1,0:T(8,128)} fusion(f32[1,512,4096]{2,1,0:T(8,128)} %collective-permute-done, f32[2,512,4096]{2,1,0:T(8,128)S(1)} %copy-done, f32[4096]{0:T(1024)S(1)} %bitcast.22, f32[512]{0:T(512)S(1)} %bitcast.23, f32[]{:T(128)} %bitcast.4), kind=kLoop, calls=%fused_computation.8 | loop fusion | flops 8388608 | bytes 25184260 | tf_op jit(solution)/shard_map/div | solution.py:59
  (6 shorter events, 0.0 us)
Async XLA Ops:
  6.5 175.4 %all-gather.2.cloned.1.call-start = ((), (), s32[]{:S(2)}) async-start(), calls=%async_computation | async-start | bytes 18874368 | tf_op jit(solution)/shard_map/all_gather | solution.py:48
  7.3 182.5 %copy-start.1 = (f32[512,1024]{1,0:T(8,128)S(1)}, f32[512,1024]{1,0:T(8,128)}, u32[]{:S(2)}) copy-start(f32[512,1024]{1,0:T(8,128)} %param.8) | copy-start | bytes 6291460
  7.3 182.5 %copy-start.2 = (s32[3]{0:T(128)S(1)}, s32[3]{0:T(128)}, u32[]{:S(2)}) copy-start(s32[3]{0:T(128)} %constant.57.clone.3) | copy-start | bytes 40
  7.3 182.5 %copy-start.3 = (s32[1024]{0:T(1024)S(1)}, s32[1024]{0:T(1024)}, u32[]{:S(2)}) copy-start(s32[1024]{0:T(1024)} %param.9) | copy-start | bytes 12292
  276.1 125.2 %copy-start = (f32[2,512,4096]{2,1,0:T(8,128)S(1)}, f32[2,512,4096]{2,1,0:T(8,128)}, u32[]{:S(2)}) copy-start(f32[2,512,4096]{2,1,0:T(8,128)} %get-tuple-element.389) | copy-start | bytes 50331652
  284.9 116.4 %collective-permute-start = (f32[1,512,4096]{2,1,0:T(8,128)}, f32[1,512,4096]{2,1,0:T(8,128)}, u32[]{:S(2)}, u32[]{:S(2)}) collective-permute-start(f32[1,512,4096]{2,1,0:T(8,128)} %slice.52), channel_id=1, source_target_pairs={{0,1},{1,2},{2,3},{3,4},{4,5},{5,6},{6,7},{7,8},{8,9},{9,10},{10,1... | collective-permute-start | bytes 25165832 | tf_op jit(solution)/shard_map/ppermute | solution.py:14
  291.3 90.9 %collective-permute-start.2 = (f32[512,1]{0,1:T(1,128)S(1)}, f32[512,1]{0,1:T(1,128)S(1)}, u32[]{:S(2)}, u32[]{:S(2)}) collective-permute-start(f32[512,1]{0,1:T(1,128)S(1)} %slice.58), channel_id=1, source_target_pairs={{0,1},{1,2},{2,3},{3,4},{4,5},{5,6},{6,7},{7,8},{8,9},{9,10},{10,1... | collective-permute-start | bytes 6152 | tf_op jit(solution)/shard_map/ppermute | solution.py:14
  294.0 86.9 %collective-permute-start.1 = (f32[1]{0:T(128)}, f32[1]{0:T(128)}, u32[]{:S(2)}, u32[]{:S(2)}) collective-permute-start(f32[1]{0:T(128)} %get-tuple-element.195), channel_id=1, source_target_pairs={{0,1},{1,2},{2,3},{3,4},{4,5},{5,6},{6,7},{7,8},{8,9},{9,10},{10,1... | collective-permute-start | bytes 20 | tf_op jit(solution)/shard_map/ppermute | solution.py:14
Sparse Core Ops, SparseCore 0:
  9.0 172.9 all-gather.1
where the time goes:
time: 422 us; the launch traced here: 415 us
  waiting for transfers between devices  260 us (62%)
  matrix products  60.6 us (14%)
  local copies, waits for them, and re-layouts  34.3 us (8%)
  blocking collectives  19.1 us (5%)
  between operations  14.8 us (4%)
  starting transfers between devices  9.11 us (2%)
  other arithmetic  9.01 us (2%)
  loops' own time  7.58 us (2%)
    all_gather x1, waiting for transfers between devices, shards(): gathered = lax.all_gather(intensity, 'frame', axis=0, tiled=True)  175 us
    ppermute x3, waiting for transfers between devices, shifted(): return lax.ppermute(block, axis, route)  84.9 us
    dot_general x3, matrix products, add_cycle(): lax.dot_general(masked, column_part, (((1,), (1,)), ((), ())), precision=...  59.5 us
    all_gather x1, blocking collectives, shards(): frame_sums = lax.all_gather(row_totals, 'frame', axis=0, tiled=True)  19.1 us
    dynamic_slice x2, local copies, waits for them, and re-layouts, add_block(): column_part = lax.dynamic_slice_in_dim(columns, block_start, block_width, 1)  15.5 us
    ppermute x3, starting transfers between devices, shifted(): return lax.ppermute(block, axis, route)  9.11 us
    slice x1, local copies, waits for them, and re-layouts, shards(): panels[own_cycles:]  8.78 us
  transfers between devices with their start and end apart: 4, of which 2 were waited for; matrix products, arithmetic and copies ran while one was open for 0% of the time, Pallas kernels for 0%

commit v1 on v0

v1 whole, which is shorter than its diff:
```python
import functools

import jax
import jax.numpy as jnp
from jax import lax
from jax.experimental import pallas as pl
from jax.experimental.pallas import tpu as pltpu
from jax.sharding import PartitionSpec as P

MESH = pl.DeviceIdType.MESH

OWN, LOW, HIGH, FAR, PAIR = range(5)
ROWS, COLS, TAIL = 512, 1024, 512
HALF = ROWS // 2
TILE = 256
DEPTH = COLS + TAIL

NT = (((1,), (1,)), ((), ()))


def kernel(
    x_ref, label_ref, out_ref,
    xm, xt, tail_label, hi, lo, row_scale, col_scale, block,
    send, recv, local,
):
    f = lax.axis_index("frame")
    r = lax.axis_index("pixel")
    a, b = f // 4, f % 4
    f_high = a * 4 + (b + 1) % 4
    f_low = a * 4 + (b + 3) % 4
    f_far = a * 4 + (b + 2) % 4
    f_pair = (1 - a) * 4 + b
    even = r % 2 == 0
    odd = r % 2 == 1
    has_next = jnp.logical_and(odd, r < 15)
    has_prev = jnp.logical_and(even, r > 0)
    high, low, pair = (f_high, r), (f_low, r), (f_pair, r)
    twin = (f, r + 1 - 2 * (r % 2))
    following = (f_pair, r + 1)
    preceding = (f_pair, r - 1)

    barrier = pltpu.get_barrier_semaphore()
    for peer in (high, low, pair, twin):
        pl.semaphore_signal(barrier, inc=1, device_id=peer, device_id_type=MESH)

    @pl.when(has_next)
    def _():
        pl.semaphore_signal(barrier, inc=1, device_id=following, device_id_type=MESH)

    @pl.when(has_prev)
    def _():
        pl.semaphore_signal(barrier, inc=1, device_id=preceding, device_id_type=MESH)

    crossing = jnp.logical_or(has_next, has_prev)

    @pl.when(crossing)
    def _():
        pl.semaphore_wait(barrier, 5)

    @pl.when(jnp.logical_not(crossing))
    def _():
        pl.semaphore_wait(barrier, 4)

    names = {}

    def remote(name, src, dst, peer):
        i = names.setdefault(name, len(names))
        return pltpu.make_async_remote_copy(src, dst, send.at[i], recv.at[i], device_id=peer, device_id_type=MESH)

    part = [pl.ds(0, HALF), pl.ds(HALF, HALF)]
    tail_cols = pl.ds(COLS - TAIL, TAIL)

    up = [remote(f"up{h}", x_ref.at[part[h]], xm.at[LOW, part[h]], high) for h in range(2)]
    down = [remote(f"down{h}", x_ref.at[part[h]], xm.at[HIGH, part[h]], low) for h in range(2)]
    across = [remote(f"across{h}", x_ref.at[part[h]], xm.at[PAIR, part[h]], pair) for h in range(2)]
    tail_out = remote("tail_out", x_ref.at[:, tail_cols], xt.at[PAIR], following)
    label_out = remote("label_out", label_ref.at[:, tail_cols], tail_label, following)
    label_twin = remote("label_twin", label_ref.at[:, tail_cols], tail_label, twin)
    tail_pair = remote("tail_pair", xt.at[PAIR], xt.at[OWN], pair)
    tail_up = remote("tail_up", xt.at[OWN], xt.at[LOW], high)
    tail_down = remote("tail_down", xt.at[OWN], xt.at[HIGH], low)
    on_up = remote("on_up", xm.at[LOW, part[0]], xm.at[FAR, part[0]], high)
    on_down = remote("on_down", xm.at[HIGH, part[1]], xm.at[FAR, part[1]], low)
    tail_on_up = remote("tail_on_up", xt.at[LOW, part[0]], xt.at[FAR, part[0]], high)
    tail_on_down = remote("tail_on_down", xt.at[HIGH, part[1]], xt.at[FAR, part[1]], low)
    twin_own = remote("twin_own", x_ref.at[:, tail_cols], xt.at[OWN], twin)
    twin_slot = {s: remote(f"twin{s}", xm.at[s, :, tail_cols], xt.at[s], twin) for s in (LOW, HIGH, PAIR)}
    twin_far = [remote(f"twin_far{h}", xm.at[FAR, part[h], tail_cols], xt.at[FAR, part[h]], twin) for h in range(2)]

    def on(cond, *acts):
        @pl.when(cond)
        def _():
            for act in acts:
                act()

    own_copy = pltpu.make_async_copy(x_ref, xm.at[OWN], local.at[0])
    on(has_next, tail_out.start, label_out.start)
    on(even, twin_own.start, label_twin.start)
    for h in range(2):
        across[h].start()
    up[0].start()
    down[1].start()
    up[1].start()
    down[0].start()
    own_copy.start()

    @pl.when(has_prev)
    def _():
        label_out.wait_recv()
        tail_out.wait_recv()
        tail_pair.start()

    @pl.when(r == 0)
    def _():
        xt[OWN] = jnp.zeros((ROWS, TAIL), jnp.float32)
        xt[PAIR] = jnp.zeros((ROWS, TAIL), jnp.float32)
        tail_label[...] = jnp.full((1, TAIL), -1, jnp.int32)

    on(has_prev, tail_pair.wait_recv)
    on(even, tail_up.start, tail_down.start)
    on(odd, twin_own.wait_recv, label_twin.wait_recv)

    keep_main = label_ref[...] == r
    keep_tail = tail_label[...] == r
    counts = jnp.sum(keep_main.astype(jnp.float32)) + jnp.sum(keep_tail.astype(jnp.float32))

    def split(slot, start=0, rows=ROWS):
        step = 64

        def body(i, _):
            at = pl.ds(pl.multiple_of(start + i * step, step), step)
            total = jnp.zeros((step, 1), jnp.float32)
            for ref, keep, base, width in ((xt, keep_tail, 0, TAIL), (xm, keep_main, TAIL, COLS)):
                v = jnp.where(keep, ref[slot, at, :], 0.0)
                v_hi = v.astype(jnp.bfloat16)
                v_lo = (v - v_hi.astype(jnp.float32)).astype(jnp.bfloat16)
                hi[slot, at, base : base + width] = v_hi
                lo[slot, at, base : base + width] = v_lo
                total = total + jnp.sum(v, axis=1, keepdims=True)
            row_scale[slot, at, :] = counts / total
            return 0

        lax.fori_loop(0, rows // step, body, 0)
        ones = jnp.ones((8, DEPTH), jnp.bfloat16)
        at = pl.ds(start, rows)
        sums = lax.dot_general(ones, hi[slot, at, :], NT, preferred_element_type=jnp.float32)
        sums += lax.dot_general(ones, lo[slot, at, :], NT, preferred_element_type=jnp.float32)
        col_scale[slot, :, at] = 1.0 / sums

    def product(row_slot, col_slot, start, cols, place):
        def body(i, _):
            at = pl.ds(pl.multiple_of(start + i * TILE, TILE), TILE)
            l_hi, l_lo = hi[row_slot], lo[row_slot]
            r_hi, r_lo = hi[col_slot, at, :], lo[col_slot, at, :]
            dot = functools.partial(lax.dot_general, dimension_numbers=NT, preferred_element_type=jnp.float32)
            total = dot(l_hi, r_hi) + (dot(l_hi, r_lo) + dot(l_lo, r_hi))
            block[place, :, at] = total * row_scale[row_slot] * col_scale[col_slot, 0:1, at]
            return 0

        lax.fori_loop(0, cols // TILE, body, 0)

    pending = []

    def keep_block(place, owner, sem):
        copy = pltpu.make_async_copy(block.at[place], out_ref.at[0, :, pl.ds(pl.multiple_of(owner * ROWS, ROWS), ROWS)], local.at[sem])
        copy.start()
        pending.append(copy)

    def give(name, place, start, cols, owner, peer):
        dst = out_ref.at[0, :, pl.ds(pl.multiple_of(owner * ROWS + start, TILE), cols)]
        copy = remote(name, block.at[place, :, pl.ds(start, cols)], dst, peer)
        copy.start()
        return copy

    own_copy.wait()
    split(OWN)
    product(OWN, OWN, 0, ROWS, 0)
    keep_block(0, f, 1)

    up[0].wait_recv()
    on_up.start()
    down[1].wait_recv()
    on_down.start()
    up[1].wait_recv()
    down[0].wait_recv()
    on(even, twin_slot[LOW].start, twin_slot[HIGH].start)
    @pl.when(even)
    def _():
        tail_up.wait_recv()
        tail_on_up.start()
        tail_down.wait_recv()
        tail_on_down.start()

    for h in range(2):
        across[h].wait_recv()
    on(even, twin_slot[PAIR].start)
    on(odd, twin_slot[LOW].wait_recv, twin_slot[HIGH].wait_recv, twin_slot[PAIR].wait_recv)
    split(PAIR)
    split(LOW)
    product(PAIR, LOW, 0, HALF, 5)
    gifts = [give("pair_low", 5, 0, HALF, f_low, pair)]
    split(HIGH)
    product(PAIR, HIGH, 0, HALF, 6)
    gifts.append(give("pair_high", 6, 0, HALF, f_high, pair))

    product(OWN, PAIR, 0, ROWS, 4)
    keep_block(4, f_pair, 2)
    product(OWN, LOW, 0, ROWS, 1)
    keep_block(1, f_low, 3)
    product(OWN, HIGH, 0, ROWS, 2)
    keep_block(2, f_high, 4)

    product(LOW, PAIR, HALF, HALF, 5)
    gifts.append(give("low_pair", 5, HALF, HALF, f_pair, low))
    product(HIGH, PAIR, HALF, HALF, 6)
    gifts.append(give("high_pair", 6, HALF, HALF, f_pair, high))

    for h, main, tail in ((0, on_up, tail_on_up), (1, on_down, tail_on_down)):
        main.wait_recv()
        on(even, twin_far[h].start, tail.wait_recv)
        on(odd, twin_far[h].wait_recv)
        split(FAR, h * HALF, HALF)
        product(PAIR, FAR, h * HALF, HALF, 7)
        gifts.append(give(f"pair_far{h}", 7, h * HALF, HALF, f_far, pair))
    product(OWN, FAR, 0, ROWS, 3)
    keep_block(3, f_far, 5)

    for copy in up + down + across + [on_up, on_down]:
        copy.wait_send()
    on(has_next, tail_out.wait_send, label_out.wait_send)
    on(has_prev, tail_pair.wait_send)
    on(
        even,
        *(c.wait_send for c in [tail_up, tail_down, tail_on_up, tail_on_down, twin_own, label_twin]),
        *(c.wait_send for c in [*twin_slot.values(), *twin_far]),
    )
    for copy in gifts:
        copy.wait()
    for copy in pending:
        copy.wait()
    assert len(names) <= SEMAPHORES


SEMAPHORES = 32


def shards(intensity, cycle_label):
    rows, cols = intensity.shape
    return pl.pallas_call(
        kernel,
        out_shape=jax.ShapeDtypeStruct((1, ROWS, 8 * ROWS), jnp.float32),
        in_specs=[pl.BlockSpec(memory_space=pl.ANY), pl.BlockSpec(memory_space=pltpu.VMEM)],
        out_specs=pl.BlockSpec(memory_space=pl.ANY),
        scratch_shapes=[
            pltpu.VMEM((5, ROWS, COLS), jnp.float32),
            pltpu.VMEM((5, ROWS, TAIL), jnp.float32),
            pltpu.VMEM((1, TAIL), jnp.int32),
            pltpu.VMEM((5, ROWS, DEPTH), jnp.bfloat16),
            pltpu.VMEM((5, ROWS, DEPTH), jnp.bfloat16),
            pltpu.VMEM((5, ROWS, 1), jnp.float32),
            pltpu.VMEM((5, 8, ROWS), jnp.float32),
            pltpu.VMEM((8, ROWS, ROWS), jnp.float32),
            pltpu.SemaphoreType.DMA((SEMAPHORES,)),
            pltpu.SemaphoreType.DMA((SEMAPHORES,)),
            pltpu.SemaphoreType.DMA((8,)),
        ],
        compiler_params=pltpu.CompilerParams(collective_id=0, has_side_effects=True, vmem_limit_bytes=56 << 20),
        name="gram_maps",
    )(intensity, cycle_label.reshape(1, cols))


def solution(mesh):
    in_specs = (P("frame", "pixel"), P("pixel"))
    out_specs = P("pixel", "frame", None)
    return jax.shard_map(shards, mesh=mesh, in_specs=in_specs, out_specs=out_specs, check_vma=False)
```

time: 422 us -> 142 us (0.34); the launches traced: 415 us -> 142 us
  waiting for transfers between devices: 260 us -> 0 us
  Pallas kernels: 0 us -> 134 us
  matrix products: 60.6 us -> 0 us
  local copies, waits for them, and re-layouts: 34.3 us -> 7.77 us
  blocking collectives: 19.1 us -> 0 us
  between operations: 14.8 us -> 0.01 us
  starting transfers between devices: 9.11 us -> 0 us
  other arithmetic: 9.01 us -> 0 us
  loops' own time: 7.58 us -> 0 us
    all_gather x1 -> x0, waiting for transfers between devices: 175 us -> none  [shards(): gathered = lax.all_gather(intensity, 'frame', axis=0, tiled=True)]
    pallas_call x0 -> x1, Pallas kernels: none -> 134 us  [shards(): pl.pallas_call(kernel, out_shape=jax.ShapeDtypeStruct((1, ROWS, 8 * ROWS)...]
    ppermute x3 -> x0, waiting for transfers between devices: 84.9 us -> none  [shifted(): return lax.ppermute(block, axis, route)]
    dot_general x4 -> x0, matrix products: 60.6 us -> none  [the longest x3 59.5 us: add_cycle(): lax.dot_general(masked, column_part, (((1,), (1,)), ((), ())), precision=...]
    all_gather x1 -> x0, blocking collectives: 19.1 us -> none  [shards(): frame_sums = lax.all_gather(row_totals, 'frame', axis=0, tiled=True)]
    dynamic_slice x6 -> x0, local copies, waits for them, and re-layouts: 15.9 us -> none  [the longest x2 15.5 us: add_block(): column_part = lax.dynamic_slice_in_dim(columns, block_start, block_width, 1)]
    slice x5 -> x0, local copies, waits for them, and re-layouts: 10.6 us -> none  [the longest x1 8.78 us: shards(): panels[own_cycles:]]
    ppermute x3 -> x0, starting transfers between devices: 9.11 us -> none  [shifted(): return lax.ppermute(block, axis, route)]
  transfers between devices with their start and end apart: 4 -> 0, of which waited for: 2 -> 0; matrix products, arithmetic and copies ran while one was open for 0% -> 0% of each run, Pallas kernels for 0% -> 0%
where the time goes in v1:
time: 142 us
  Pallas kernels  134 us (94%)
  local copies, waits for them, and re-layouts  7.77 us (5%)
    pallas_call x1, Pallas kernels, shards(): pl.pallas_call(kernel, out_shape=jax.ShapeDtypeStruct((1, ROWS, 8 * ROWS)...  134 us
    unnamed x1, local copies, waits for them, and re-layouts  7.77 us

profile of v1, /device:TPU:7, one launch (start us, length us, event | category | flops | bytes accessed | tf_op | source)
XLA Modules:
  0.0 141.8 jit_solution(9900055809017867631)
XLA Ops:
  0.0 134.0 %gram_maps.1 = f32[1,512,4096]{2,1,0:T(8,128)} custom-call(f32[512,1024]{1,0:T(8,128)} %x_ref.1, s32[1,1024]{1,0:T(1,128)} %bitcast.1), custom_call_target="tpu_custom_call" | custom-call | tf_op jit(solution)/shard_map/gram_maps/pallas_call | solution.py:249
  134.0 7.8 %copy.4 = f32[1,512,4096]{2,1,0:T(8,128)} copy(f32[1,512,4096]{2,1,0:T(8,128)} %gram_maps.1) | data formatting | bytes 16777216

commit v2 on v1

v2 whole, which is shorter than its diff:
```python
import functools

import jax
import jax.numpy as jnp
from jax import lax
from jax.experimental import pallas as pl
from jax.experimental.pallas import tpu as pltpu
from jax.sharding import PartitionSpec as P

MESH = pl.DeviceIdType.MESH

OWN, LOW, HIGH, FAR, PAIR = range(5)
ROWS, COLS, TAIL = 512, 1024, 512
HALF = ROWS // 2
CHUNK = ROWS // 4
TILE = 256
DEPTH = COLS + TAIL

NT = (((1,), (1,)), ((), ()))


def kernel(
    x_ref, label_hbm, out_ref,
    xm, xt, label_ref, tail_label, hi, lo, row_scale, col_scale, inverse, block,
    send, recv, local,
):
    f = lax.axis_index("frame")
    r = lax.axis_index("pixel")
    a, b = f // 4, f % 4
    f_high = a * 4 + (b + 1) % 4
    f_low = a * 4 + (b + 3) % 4
    f_far = a * 4 + (b + 2) % 4
    f_pair = (1 - a) * 4 + b
    even = r % 2 == 0
    odd = r % 2 == 1
    has_next = jnp.logical_and(odd, r < 15)
    has_prev = jnp.logical_and(even, r > 0)
    high, low, pair = (f_high, r), (f_low, r), (f_pair, r)
    twin = (f, r + 1 - 2 * (r % 2))
    following = (f_pair, r + 1)
    preceding = (f_pair, r - 1)

    barrier = pltpu.get_barrier_semaphore()
    for peer in (high, low, pair, twin):
        pl.semaphore_signal(barrier, inc=1, device_id=peer, device_id_type=MESH)

    @pl.when(has_next)
    def _():
        pl.semaphore_signal(barrier, inc=1, device_id=following, device_id_type=MESH)

    @pl.when(has_prev)
    def _():
        pl.semaphore_signal(barrier, inc=1, device_id=preceding, device_id_type=MESH)

    crossing = jnp.logical_or(has_next, has_prev)

    @pl.when(crossing)
    def _():
        pl.semaphore_wait(barrier, 5)

    @pl.when(jnp.logical_not(crossing))
    def _():
        pl.semaphore_wait(barrier, 4)

    names = {}

    def remote(name, src, dst, peer):
        i = names.setdefault(name, len(names))
        return pltpu.make_async_remote_copy(src, dst, send.at[i], recv.at[i], device_id=peer, device_id_type=MESH)

    part = [pl.ds(0, HALF), pl.ds(HALF, HALF)]
    chunk = [pl.ds(i * CHUNK, CHUNK) for i in range(ROWS // CHUNK)]
    tail_cols = pl.ds(COLS - TAIL, TAIL)
    head_cols = pl.ds(0, COLS - TAIL)

    up = [remote(f"up{h}", x_ref.at[part[h]], xm.at[LOW, part[h]], high) for h in range(2)]
    down = [remote(f"down{h}", x_ref.at[part[h]], xm.at[HIGH, part[h]], low) for h in range(2)]
    across = [
        remote(f"across{h}", x_ref.at[part[h], tail_cols], xm.at[PAIR, part[h], tail_cols], pair) for h in range(2)
    ] + [remote("across2", x_ref.at[:, head_cols], xm.at[PAIR, :, head_cols], pair)]
    tail_out = remote("tail_out", x_ref.at[:, tail_cols], xt.at[PAIR], following)
    relay = [
        remote(f"relay{h}", xm.at[PAIR, part[h], tail_cols], xt.at[OWN, part[h]], following) for h in range(2)
    ]
    label_out = remote("label_out", label_hbm.at[:, tail_cols], tail_label, following)
    label_twin = remote("label_twin", label_hbm.at[:, tail_cols], tail_label, twin)
    tail_up = remote("tail_up", xt.at[OWN], xt.at[LOW], high)
    tail_down = remote("tail_down", xt.at[OWN], xt.at[HIGH], low)
    far_from = [(LOW, high), (LOW, high), (HIGH, low), (HIGH, low)]
    far = [
        remote(f"far{i}", xm.at[slot, chunk[i]], xm.at[FAR, chunk[i]], peer) for i, (slot, peer) in enumerate(far_from)
    ]
    tail_far = [
        remote(f"tail_far{i}", xt.at[slot, chunk[i]], xt.at[FAR, chunk[i]], peer)
        for i, (slot, peer) in enumerate(far_from)
    ]
    twin_own = remote("twin_own", x_ref.at[:, tail_cols], xt.at[OWN], twin)
    twin_slot = {s: remote(f"twin{s}", xm.at[s, :, tail_cols], xt.at[s], twin) for s in (LOW, HIGH, PAIR)}
    twin_far = [remote(f"twin_far{i}", xm.at[FAR, chunk[i], tail_cols], xt.at[FAR, chunk[i]], twin) for i in range(4)]

    def on(cond, *acts):
        @pl.when(cond)
        def _():
            for act in acts:
                act()

    own_copy = pltpu.make_async_copy(x_ref, xm.at[OWN], local.at[0])
    label_copy = pltpu.make_async_copy(label_hbm, label_ref, local.at[1])
    label_copy.start()
    on(has_next, tail_out.start, label_out.start)
    on(even, twin_own.start, label_twin.start)
    for h in range(3):
        across[h].start()
    up[0].start()
    down[1].start()
    up[1].start()
    down[0].start()
    own_copy.start()

    @pl.when(has_prev)
    def _():
        label_out.wait_recv()

    on(odd, label_twin.wait_recv)
    label_copy.wait()

    @pl.when(r == 0)
    def _():
        xt[OWN] = jnp.zeros((ROWS, TAIL), jnp.float32)
        xt[PAIR] = jnp.zeros((ROWS, TAIL), jnp.float32)
        tail_label[...] = jnp.full((1, TAIL), -1, jnp.int32)

    keep_main = label_ref[...] == r
    keep_tail = tail_label[...] == r
    counts = jnp.sum(keep_main.astype(jnp.float32)) + jnp.sum(keep_tail.astype(jnp.float32))

    def split(slot, start=0, rows=ROWS, place=None):
        step = 64
        place = start if place is None else place

        def body(i, _):
            at = pl.ds(pl.multiple_of(start + i * step, step), step)
            to = pl.ds(pl.multiple_of(place + i * step, step), step)
            total = jnp.zeros((step, 1), jnp.float32)
            for ref, keep, base, width in ((xt, keep_tail, 0, TAIL), (xm, keep_main, TAIL, COLS)):
                v = jnp.where(keep, ref[slot, at, :], 0.0)
                v_hi = v.astype(jnp.bfloat16)
                v_lo = (v - v_hi.astype(jnp.float32)).astype(jnp.bfloat16)
                hi[slot, to, base : base + width] = v_hi
                lo[slot, to, base : base + width] = v_lo
                total = total + jnp.sum(v, axis=1, keepdims=True)
            row_scale[slot, to, :] = counts / total
            inverse[to, :] = jnp.broadcast_to(1.0 / total, (step, 128))
            return 0

        lax.fori_loop(0, rows // step, body, 0)
        for i in range(rows // 128):
            to = pl.ds(place + i * 128, 128)
            col_scale[slot, :, to] = inverse[to, :].T[0:8, :]

    def product(row_slot, col_slot, start, cols, place, place_start):
        tile = min(cols, TILE)

        def body(i, _):
            at = pl.ds(pl.multiple_of(start + i * tile, tile), tile)
            to = pl.ds(pl.multiple_of(place_start + i * tile, tile), tile)
            l_hi, l_lo = hi[row_slot], lo[row_slot]
            r_hi, r_lo = hi[col_slot, at, :], lo[col_slot, at, :]
            dot = functools.partial(lax.dot_general, dimension_numbers=NT, preferred_element_type=jnp.float32)
            total = dot(l_hi, r_hi) + (dot(l_hi, r_lo) + dot(l_lo, r_hi))
            total = total * row_scale[row_slot] * col_scale[col_slot, 0:1, at]
            if col_slot == FAR:
                for half in range(2):
                    to = pl.ds(pl.multiple_of(place_start + half * HALF + i * CHUNK, CHUNK), CHUNK)
                    place[:, to] = total[:, half * CHUNK : (half + 1) * CHUNK]
            else:
                place[:, to] = total
            return 0

        lax.fori_loop(0, cols // tile, body, 0)

    def keep(slot, owner):
        product(OWN, slot, 0, ROWS, out_ref.at[0], owner * ROWS)

    gifts = []

    def hand(place, start, cols, owner, peer):
        dst = out_ref.at[0, :, pl.ds(pl.multiple_of(owner * ROWS + start, CHUNK), cols)]
        copy = remote(f"gift{len(gifts)}", block.at[place, :, pl.ds(start, cols)], dst, peer)
        gifts.append(copy)
        return copy

    def make(row_slot, col_slot, start, cols, place, owner, peer):
        product(row_slot, col_slot, start, cols, block.at[place], start)
        return hand(place, start, cols, owner, peer)

    own_copy.wait()
    on(odd, twin_own.wait_recv)

    @pl.when(has_prev)
    def _():
        tail_out.wait_recv()
        for h in range(2):
            relay[h].wait_recv()

    on(even, tail_up.start, tail_down.start)
    split(OWN)
    keep(OWN, f)

    for h in range(2):
        across[h].wait_recv()

        @pl.when(has_next)
        def _(h=h):
            relay[h].start()

    for h in range(2):
        up[h].wait_recv()
    on(even, twin_slot[LOW].start)
    across[2].wait_recv()
    on(even, twin_slot[PAIR].start)
    for h in range(2):
        down[h].wait_recv()
    on(even, twin_slot[HIGH].start)

    @pl.when(even)
    def _():
        far[0].start()
        far[2].start()

    on(odd, twin_slot[PAIR].wait_recv)
    split(PAIR)

    @pl.when(even)
    def _():
        tail_up.wait_recv()
        tail_far[0].start()
        far[1].start()
        tail_far[1].start()
        tail_down.wait_recv()
        tail_far[2].start()
        far[3].start()
        tail_far[3].start()

    on(odd, twin_slot[LOW].wait_recv)
    split(LOW)
    make(PAIR, LOW, 0, HALF, 0, f_low, pair).start()
    on(odd, twin_slot[HIGH].wait_recv)
    split(HIGH)
    make(PAIR, HIGH, 0, HALF, 1, f_high, pair).start()

    @pl.when(odd)
    def _():
        for i in (0, 2, 1, 3):
            far[i].start()

    below = make(LOW, PAIR, HALF, HALF, 0, f_pair, low)
    above = make(HIGH, PAIR, HALF, HALF, 1, f_pair, high)
    on(even, below.start, above.start)
    keep(PAIR, f_pair)
    keep(LOW, f_low)
    keep(HIGH, f_high)

    for n in range(2):
        for half in range(2):
            i = n + 2 * half
            far[i].wait_recv()
            on(even, twin_far[i].start, tail_far[i].wait_recv)
            on(odd, twin_far[i].wait_recv)
            split(FAR, i * CHUNK, CHUNK, n * HALF + half * CHUNK)
        if n == 1:
            on(odd, below.start, above.start)
        product(PAIR, FAR, n * HALF, HALF, block.at[2], n * CHUNK)
        for half in range(2):
            hand(2, half * HALF + n * CHUNK, CHUNK, f_far, pair).start()
    keep(FAR, f_far)

    for copy in up + down + across + far:
        copy.wait_send()
    on(has_next, tail_out.wait_send, label_out.wait_send, relay[0].wait_send, relay[1].wait_send)
    on(
        even,
        *(c.wait_send for c in [tail_up, tail_down, twin_own, label_twin]),
        *(c.wait_send for c in [*tail_far, *twin_slot.values(), *twin_far]),
    )
    for copy in gifts:
        copy.wait()
    assert len(names) <= SEMAPHORES


SEMAPHORES = 48


def shards(intensity, cycle_label):
    rows, cols = intensity.shape
    return pl.pallas_call(
        kernel,
        out_shape=pltpu.VMEM((1, ROWS, 8 * ROWS), jnp.float32),
        in_specs=[pl.BlockSpec(memory_space=pltpu.HBM), pl.BlockSpec(memory_space=pltpu.HBM)],
        out_specs=pl.BlockSpec(memory_space=pltpu.VMEM),
        scratch_shapes=[
            pltpu.VMEM((5, ROWS, COLS), jnp.float32),
            pltpu.VMEM((5, ROWS, TAIL), jnp.float32),
            pltpu.VMEM((1, COLS), jnp.int32),
            pltpu.VMEM((1, TAIL), jnp.int32),
            pltpu.VMEM((5, ROWS, DEPTH), jnp.bfloat16),
            pltpu.VMEM((5, ROWS, DEPTH), jnp.bfloat16),
            pltpu.VMEM((5, ROWS, 1), jnp.float32),
            pltpu.VMEM((5, 8, ROWS), jnp.float32),
            pltpu.VMEM((ROWS, 128), jnp.float32),
            pltpu.VMEM((3, ROWS, ROWS), jnp.float32),
            pltpu.SemaphoreType.DMA((SEMAPHORES,)),
            pltpu.SemaphoreType.DMA((SEMAPHORES,)),
            pltpu.SemaphoreType.DMA((2,)),
        ],
        compiler_params=pltpu.CompilerParams(collective_id=0, has_side_effects=True, vmem_limit_bytes=55 << 20),
        name="gram_maps",
    )(intensity, cycle_label.reshape(1, cols))


def solution(mesh):
    in_specs = (P("frame", "pixel"), P("pixel"))
    out_specs = P("pixel", "frame", None)
    return jax.shard_map(shards, mesh=mesh, in_specs=in_specs, out_specs=out_specs, check_vma=False)
```

time: 142 us -> 115 us (0.81)
  Pallas kernels: 134 us -> 111 us
  local copies, waits for them, and re-layouts: 7.77 us -> 3.4 us
    pallas_call x1, Pallas kernels: 134 us -> 111 us  [shards(): pl.pallas_call(kernel, out_shape=pltpu.VMEM((1, ROWS, 8 * ROWS), jnp.floa...]
    unnamed x1, local copies, waits for them, and re-layouts: 7.77 us -> 3.4 us
where the time goes in v2:
time: 115 us
  Pallas kernels  111 us (97%)
  local copies, waits for them, and re-layouts  3.4 us (3%)
    pallas_call x1, Pallas kernels, shards(): pl.pallas_call(kernel, out_shape=pltpu.VMEM((1, ROWS, 8 * ROWS), jnp.floa...  111 us
    unnamed x1, local copies, waits for them, and re-layouts  3.4 us

profile of v2, /device:TPU:7, one launch (start us, length us, event | category | flops | bytes accessed | tf_op | source)
XLA Modules:
  0.0 114.7 jit_solution(8322674499872660616)
XLA Ops:
  0.0 111.3 %gram_maps.1 = f32[1,512,4096]{2,1,0:T(8,128)S(1)} custom-call(f32[512,1024]{1,0:T(8,128)} %x_ref.1, s32[1,1024]{1,0:T(1,128)} %bitcast.1), custom_call_target="tpu_custom_call" | custom-call | tf_op jit(solution)/shard_map/gram_maps/pallas_call | solution.py:296
  111.3 3.4 %copy.4 = f32[1,512,4096]{2,1,0:T(8,128)} copy(f32[1,512,4096]{2,1,0:T(8,128)S(1)} %gram_maps.1) | data formatting | bytes 16777216

commit v3 on v2

v3 whole, which is shorter than its diff:
```python
import functools

import jax
import jax.numpy as jnp
from jax import lax
from jax.experimental import pallas as pl
from jax.experimental.pallas import tpu as pltpu
from jax.sharding import PartitionSpec as P

MESH = pl.DeviceIdType.MESH

OWN, NEXT, FAR, PAIR = range(4)
ROWS, COLS, TAIL = 512, 1024, 512
HALF = ROWS // 2
TILE = 256
DEPTH = COLS + TAIL

NT = (((1,), (1,)), ((), ()))


def kernel(
    x_ref, label_hbm, out_ref,
    xm, xt, label_ref, tail_label, hi, lo, row_scale, col_scale, inverse, block,
    send, recv, local, go,
):
    f = lax.axis_index("frame")
    r = lax.axis_index("pixel")
    a, b = f // 4, f % 4
    turn = 2 * (r % 2)
    f_next = a * 4 + (b + 1 + turn) % 4
    f_last = a * 4 + (b + 3 - turn) % 4
    f_far = a * 4 + (b + 2) % 4
    f_pair = (1 - a) * 4 + b
    even = r % 2 == 0
    odd = r % 2 == 1
    has_next = jnp.logical_and(odd, r < 15)
    has_prev = jnp.logical_and(even, r > 0)
    nxt, last, pair = (f_next, r), (f_last, r), (f_pair, r)
    twin = (f, r + 1 - turn)
    following = (f_pair, r + 1)
    preceding = (f_pair, r - 1)

    barrier = pltpu.get_barrier_semaphore()
    for peer in (nxt, last, pair, twin):
        pl.semaphore_signal(barrier, inc=1, device_id=peer, device_id_type=MESH)

    @pl.when(has_next)
    def _():
        pl.semaphore_signal(barrier, inc=1, device_id=following, device_id_type=MESH)

    @pl.when(has_prev)
    def _():
        pl.semaphore_signal(barrier, inc=1, device_id=preceding, device_id_type=MESH)

    crossing = jnp.logical_or(has_next, has_prev)

    @pl.when(crossing)
    def _():
        pl.semaphore_wait(barrier, 5)

    @pl.when(jnp.logical_not(crossing))
    def _():
        pl.semaphore_wait(barrier, 4)

    names = {}

    def remote(name, src, dst, peer):
        i = names.setdefault(name, len(names))
        return pltpu.make_async_remote_copy(src, dst, send.at[i], recv.at[i], device_id=peer, device_id_type=MESH)

    part = [pl.ds(0, HALF), pl.ds(HALF, HALF)]
    tail_cols = pl.ds(COLS - TAIL, TAIL)
    head_cols = pl.ds(0, COLS - TAIL)

    along = [remote(f"along{h}", x_ref.at[part[h]], xm.at[NEXT, part[h]], last) for h in range(2)]
    far = [remote(f"far{h}", xm.at[NEXT, part[h]], xm.at[FAR, part[h]], last) for h in range(2)]
    tail_along = remote("tail_along", xt.at[OWN], xt.at[NEXT], last)
    tail_far = [remote(f"tail_far{h}", xt.at[NEXT, part[h]], xt.at[FAR, part[h]], last) for h in range(2)]
    across = [
        remote(f"across{c}{h}", x_ref.at[part[h], cols], xm.at[PAIR, part[h], cols], pair)
        for c, cols in enumerate((tail_cols, head_cols))
        for h in range(2)
    ]
    tail_out = remote("tail_out", x_ref.at[:, tail_cols], xt.at[PAIR], following)
    relay = [
        remote(f"relay{h}", xm.at[PAIR, part[h], tail_cols], xt.at[OWN, part[h]], following) for h in range(2)
    ]
    label_out = remote("label_out", label_hbm.at[:, tail_cols], tail_label, following)
    label_twin = remote("label_twin", label_hbm.at[:, tail_cols], tail_label, twin)
    twin_own = remote("twin_own", x_ref.at[:, tail_cols], xt.at[OWN], twin)
    twin_pair, twin_far = (
        [remote(f"twin{s}{h}", xm.at[s, part[h], tail_cols], xt.at[s, part[h]], twin) for h in range(2)]
        for s in (PAIR, FAR)
    )

    def on(cond, *acts):
        @pl.when(cond)
        def _():
            for act in acts:
                act()

    own_copy = pltpu.make_async_copy(x_ref, xm.at[OWN], local.at[0])
    label_copy = pltpu.make_async_copy(label_hbm, label_ref, local.at[1])
    label_copy.start()
    on(has_next, tail_out.start, label_out.start)
    on(even, twin_own.start, label_twin.start)
    for h in range(4):
        across[h].start()
    for h in range(2):
        along[h].start()
    own_copy.start()

    @pl.when(has_prev)
    def _():
        label_out.wait_recv()

    on(odd, label_twin.wait_recv)
    label_copy.wait()

    @pl.when(r == 0)
    def _():
        xt[OWN] = jnp.zeros((ROWS, TAIL), jnp.float32)
        xt[PAIR] = jnp.zeros((ROWS, TAIL), jnp.float32)
        tail_label[...] = jnp.full((1, TAIL), -1, jnp.int32)

    keep_main = label_ref[...] == r
    keep_tail = tail_label[...] == r
    counts = jnp.sum(keep_main.astype(jnp.float32)) + jnp.sum(keep_tail.astype(jnp.float32))

    def split(slot, start=0, rows=ROWS, place=None):
        step = 64
        place = start if place is None else place

        def body(i, _):
            at = pl.ds(pl.multiple_of(start + i * step, step), step)
            to = pl.ds(pl.multiple_of(place + i * step, step), step)
            total = jnp.zeros((step, 1), jnp.float32)
            for ref, keep, base, width in ((xt, keep_tail, 0, TAIL), (xm, keep_main, TAIL, COLS)):
                v = jnp.where(keep, ref[slot, at, :], 0.0)
                v_hi = v.astype(jnp.bfloat16)
                v_lo = (v - v_hi.astype(jnp.float32)).astype(jnp.bfloat16)
                hi[slot, to, base : base + width] = v_hi
                lo[slot, to, base : base + width] = v_lo
                total = total + jnp.sum(v, axis=1, keepdims=True)
            row_scale[slot, to, :] = counts / total
            inverse[to, :] = jnp.broadcast_to(1.0 / total, (step, 128))
            return 0

        lax.fori_loop(0, rows // step, body, 0)
        for i in range(rows // 128):
            to = pl.ds(place + i * 128, 128)
            col_scale[slot, :, to] = inverse[to, :].T[0:8, :]

    def product(row_slot, col_slot, place, place_start, start=0, rows=ROWS):
        def body(i, _):
            at = pl.ds(pl.multiple_of(i * TILE, TILE), TILE)
            to = pl.ds(pl.multiple_of(place_start + i * TILE, TILE), TILE)
            up = pl.ds(start, rows)
            l_hi, l_lo = hi[row_slot, up, :], lo[row_slot, up, :]
            r_hi, r_lo = hi[col_slot, at, :], lo[col_slot, at, :]
            dot = functools.partial(lax.dot_general, dimension_numbers=NT, preferred_element_type=jnp.float32)
            total = dot(l_hi, r_hi) + (dot(l_hi, r_lo) + dot(l_lo, r_hi))
            place[up, to] = total * row_scale[row_slot, up, :] * col_scale[col_slot, 0:1, at]
            return 0

        lax.fori_loop(0, ROWS // TILE, body, 0)

    def keep(slot, owner):
        product(OWN, slot, out_ref.at[0], owner * ROWS)

    gifts = []

    def make(place, row_slot, col_slot, owner, peer, start=0, rows=ROWS):
        product(row_slot, col_slot, block.at[place], 0, start, rows)
        up = pl.ds(start, rows)
        dst = out_ref.at[0, up, pl.ds(pl.multiple_of(owner * ROWS, ROWS), ROWS)]
        copy = remote(f"gift{len(gifts)}", block.at[place, up], dst, peer)
        gifts.append(copy)
        return copy

    own_copy.wait()

    @pl.when(odd)
    def _():
        twin_own.wait_recv()
        tail_along.start()
        for h in range(2):
            across[h].wait_recv()

            @pl.when(has_next)
            def _(h=h):
                relay[h].start()

            along[h].wait_recv()
            far[h].start()

    @pl.when(even)
    def _():
        for h in range(2):
            across[h].wait_recv()
            twin_pair[h].start()
        along[0].wait_recv()
        far[0].start()

        @pl.when(has_prev)
        def _():
            tail_out.wait_recv()
            for h in range(2):
                relay[h].wait_recv()

        tail_along.start()
        along[1].wait_recv()
        far[1].start()

    split(OWN)
    keep(OWN, f)

    across[2].wait_recv()
    on(odd, twin_pair[0].wait_recv)
    split(PAIR, 0, HALF)
    tail_along.wait_recv()
    on(even, tail_far[0].start, tail_far[1].start)
    split(NEXT)
    make(0, PAIR, NEXT, f_next, pair, 0, HALF).start()
    across[3].wait_recv()
    on(odd, twin_pair[1].wait_recv)
    split(PAIR, HALF, HALF)
    make(0, PAIR, NEXT, f_next, pair, HALF, HALF).start()

    near = [make(2, NEXT, OWN, f, nxt)]
    on(even, near[0].start)
    near.append(make(3, NEXT, PAIR, f_pair, nxt))
    on(even, near[1].start)
    keep(PAIR, f_pair)

    for h in range(2):
        far[h].wait_recv()
        on(even, twin_far[h].start)
    keep(NEXT, f_next)
    for h in range(2):
        on(odd, twin_far[h].wait_recv)

        @pl.when(even)
        def _(h=h):
            tail_far[h].wait_recv()
            if h == GO_AT:
                pl.semaphore_signal(go, inc=1, device_id=twin, device_id_type=MESH)

        split(FAR, h * HALF, HALF)
    make(1, PAIR, FAR, f_far, pair).start()

    @pl.when(odd)
    def _():
        pl.semaphore_wait(go, 1)
        for copy in near:
            copy.start()

    keep(FAR, f_far)

    for copy in along + far + across + [tail_along]:
        copy.wait_send()
    on(has_next, tail_out.wait_send, label_out.wait_send, relay[0].wait_send, relay[1].wait_send)
    on(even, *(c.wait_send for c in [*tail_far, *twin_pair, *twin_far, twin_own, label_twin]))
    for copy in gifts:
        copy.wait()
    assert len(names) <= SEMAPHORES


SEMAPHORES = 32
GO_AT = 0


def shards(intensity, cycle_label):
    rows, cols = intensity.shape
    return pl.pallas_call(
        kernel,
        out_shape=pltpu.VMEM((1, ROWS, 8 * ROWS), jnp.float32),
        in_specs=[pl.BlockSpec(memory_space=pltpu.HBM), pl.BlockSpec(memory_space=pltpu.HBM)],
        out_specs=pl.BlockSpec(memory_space=pltpu.VMEM),
        scratch_shapes=[
            pltpu.VMEM((4, ROWS, COLS), jnp.float32),
            pltpu.VMEM((4, ROWS, TAIL), jnp.float32),
            pltpu.VMEM((1, COLS), jnp.int32),
            pltpu.VMEM((1, TAIL), jnp.int32),
            pltpu.VMEM((4, ROWS, DEPTH), jnp.bfloat16),
            pltpu.VMEM((4, ROWS, DEPTH), jnp.bfloat16),
            pltpu.VMEM((4, ROWS, 1), jnp.float32),
            pltpu.VMEM((4, 8, ROWS), jnp.float32),
            pltpu.VMEM((ROWS, 128), jnp.float32),
            pltpu.VMEM((4, ROWS, ROWS), jnp.float32),
            pltpu.SemaphoreType.DMA((SEMAPHORES,)),
            pltpu.SemaphoreType.DMA((SEMAPHORES,)),
            pltpu.SemaphoreType.DMA((2,)),
            pltpu.SemaphoreType.REGULAR,
        ],
        compiler_params=pltpu.CompilerParams(collective_id=0, has_side_effects=True, vmem_limit_bytes=55 << 20),
        name="gram_maps",
    )(intensity, cycle_label.reshape(1, cols))


def solution(mesh):
    in_specs = (P("frame", "pixel"), P("pixel"))
    out_specs = P("pixel", "frame", None)
    return jax.shard_map(shards, mesh=mesh, in_specs=in_specs, out_specs=out_specs, check_vma=False)
```

time: 115 us -> 103 us (0.90)
  Pallas kernels: 111 us -> 99.2 us
    pallas_call x1, Pallas kernels: 111 us -> 99.2 us  [shards(): pl.pallas_call(kernel, out_shape=pltpu.VMEM((1, ROWS, 8 * ROWS), jnp.floa...]
where the time goes in v3:
time: 103 us
  Pallas kernels  99.2 us (96%)
  local copies, waits for them, and re-layouts  3.4 us (3%)
    pallas_call x1, Pallas kernels, shards(): pl.pallas_call(kernel, out_shape=pltpu.VMEM((1, ROWS, 8 * ROWS), jnp.floa...  99.2 us
    unnamed x1, local copies, waits for them, and re-layouts  3.4 us

profile of v3, /device:TPU:7, one launch (start us, length us, event | category | flops | bytes accessed | tf_op | source)
XLA Modules:
  0.0 102.6 jit_solution(18352972065064041009)
XLA Ops:
  0.0 99.2 %gram_maps.1 = f32[1,512,4096]{2,1,0:T(8,128)S(1)} custom-call(f32[512,1024]{1,0:T(8,128)} %x_ref.1, s32[1,1024]{1,0:T(1,128)} %bitcast.1), custom_call_target="tpu_custom_call" | custom-call | tf_op jit(solution)/shard_map/gram_maps/pallas_call | solution.py:275
  99.2 3.4 %copy.4 = f32[1,512,4096]{2,1,0:T(8,128)} copy(f32[1,512,4096]{2,1,0:T(8,128)S(1)} %gram_maps.1) | data formatting | bytes 16777216

commit v4 on v3

--- a/solution.py
+++ b/solution.py
@@ -20,7 +20,7 @@
 
 def kernel(
     x_ref, label_hbm, out_ref,
-    xm, xt, label_ref, tail_label, hi, lo, row_scale, col_scale, inverse, block,
+    xm, xt, passing, label_ref, tail_label, hi, lo, row_scale, col_scale, inverse, block,
     send, recv, local, go,
 ):
     f = lax.axis_index("frame")
@@ -69,13 +69,17 @@
         return pltpu.make_async_remote_copy(src, dst, send.at[i], recv.at[i], device_id=peer, device_id_type=MESH)
 
     part = [pl.ds(0, HALF), pl.ds(HALF, HALF)]
+    around = pl.ds(0, AROUND)
+    rest = [pl.ds(AROUND, HALF - AROUND), pl.ds(HALF, HALF)]
     tail_cols = pl.ds(COLS - TAIL, TAIL)
     head_cols = pl.ds(0, COLS - TAIL)
 
     along = [remote(f"along{h}", x_ref.at[part[h]], xm.at[NEXT, part[h]], last) for h in range(2)]
     far = [remote(f"far{h}", xm.at[NEXT, part[h]], xm.at[FAR, part[h]], last) for h in range(2)]
     tail_along = remote("tail_along", xt.at[OWN], xt.at[NEXT], last)
-    tail_far = [remote(f"tail_far{h}", xt.at[NEXT, part[h]], xt.at[FAR, part[h]], last) for h in range(2)]
+    tail_far = [remote(f"tail_far{h}", xt.at[NEXT, p], xt.at[FAR, p], last) for h, p in enumerate(rest)]
+    round_one = remote("round_one", xt.at[OWN, around], passing, nxt)
+    round_two = remote("round_two", passing, xt.at[FAR, around], nxt)
     across = [
         remote(f"across{c}{h}", x_ref.at[part[h], cols], xm.at[PAIR, part[h], cols], pair)
         for c, cols in enumerate((tail_cols, head_cols))
@@ -151,10 +155,10 @@
             to = pl.ds(place + i * 128, 128)
             col_scale[slot, :, to] = inverse[to, :].T[0:8, :]
 
-    def product(row_slot, col_slot, place, place_start, start=0, rows=ROWS):
+    def product(row_slot, col_slot, place, place_start, start=0, rows=ROWS, col=0, cols=ROWS):
         def body(i, _):
-            at = pl.ds(pl.multiple_of(i * TILE, TILE), TILE)
-            to = pl.ds(pl.multiple_of(place_start + i * TILE, TILE), TILE)
+            at = pl.ds(pl.multiple_of(col + i * TILE, TILE), TILE)
+            to = pl.ds(pl.multiple_of(place_start + col + i * TILE, TILE), TILE)
             up = pl.ds(start, rows)
             l_hi, l_lo = hi[row_slot, up, :], lo[row_slot, up, :]
             r_hi, r_lo = hi[col_slot, at, :], lo[col_slot, at, :]
@@ -163,18 +167,18 @@
             place[up, to] = total * row_scale[row_slot, up, :] * col_scale[col_slot, 0:1, at]
             return 0
 
-        lax.fori_loop(0, ROWS // TILE, body, 0)
+        lax.fori_loop(0, cols // TILE, body, 0)
 
     def keep(slot, owner):
         product(OWN, slot, out_ref.at[0], owner * ROWS)
 
     gifts = []
 
-    def make(place, row_slot, col_slot, owner, peer, start=0, rows=ROWS):
-        product(row_slot, col_slot, block.at[place], 0, start, rows)
+    def make(place, row_slot, col_slot, owner, peer, start=0, rows=ROWS, col=0, cols=ROWS):
+        product(row_slot, col_slot, block.at[place], 0, start, rows, col, cols)
         up = pl.ds(start, rows)
-        dst = out_ref.at[0, up, pl.ds(pl.multiple_of(owner * ROWS, ROWS), ROWS)]
-        copy = remote(f"gift{len(gifts)}", block.at[place, up], dst, peer)
+        dst = out_ref.at[0, up, pl.ds(pl.multiple_of(owner * ROWS + col, TILE), cols)]
+        copy = remote(f"gift{len(gifts)}", block.at[place, up, pl.ds(col, cols)], dst, peer)
         gifts.append(copy)
         return copy
 
@@ -196,11 +200,11 @@
 
     @pl.when(even)
     def _():
+        along[0].wait_recv()
+        far[0].start()
         for h in range(2):
             across[h].wait_recv()
             twin_pair[h].start()
-        along[0].wait_recv()
-        far[0].start()
 
         @pl.when(has_prev)
         def _():
@@ -209,6 +213,7 @@
                 relay[h].wait_recv()
 
         tail_along.start()
+        round_one.start()
         along[1].wait_recv()
         far[1].start()
 
@@ -219,55 +224,77 @@
     on(odd, twin_pair[0].wait_recv)
     split(PAIR, 0, HALF)
     tail_along.wait_recv()
-    on(even, tail_far[0].start, tail_far[1].start)
+    on(even, tail_far[0].start, tail_far[1].start, round_one.wait_recv, round_two.start)
     split(NEXT)
     make(0, PAIR, NEXT, f_next, pair, 0, HALF).start()
+
+    @pl.when(even)
+    def _():
+        far[0].wait_recv()
+        twin_far[0].start()
+
+    keep(NEXT, f_next)
+    near = make(2, NEXT, OWN, f, nxt)
     across[3].wait_recv()
     on(odd, twin_pair[1].wait_recv)
     split(PAIR, HALF, HALF)
     make(0, PAIR, NEXT, f_next, pair, HALF, HALF).start()
 
-    near = [make(2, NEXT, OWN, f, nxt)]
-    on(even, near[0].start)
-    near.append(make(3, NEXT, PAIR, f_pair, nxt))
-    on(even, near[1].start)
+    far_gift = [None, None]
+
+    def far_half(h):
+        split(FAR, h * HALF, HALF)
+        product(PAIR, FAR, block.at[1], 0, 0, ROWS, h * HALF, HALF)
+        far_gift[h].start()
+
+    for h in range(2):
+        dst = out_ref.at[0, :, pl.ds(pl.multiple_of(f_far * ROWS + h * HALF, TILE), HALF)]
+        far_gift[h] = remote(f"far_gift{h}", block.at[1, :, pl.ds(h * HALF, HALF)], dst, pair)
+    gifts.extend(far_gift)
+
+    @pl.when(odd)
+    def _():
+        far[0].wait_recv()
+        twin_far[0].wait_recv()
+        far_half(0)
+        pl.semaphore_wait(go, 1)
+
+    @pl.when(even)
+    def _():
+        far[1].wait_recv()
+        twin_far[1].start()
+        tail_far[0].wait_recv()
+        pl.semaphore_signal(go, inc=1, device_id=twin, device_id_type=MESH)
+
+    near.start()
+    make(3, NEXT, PAIR, f_pair, nxt).start()
+
+    @pl.when(even)
+    def _():
+        round_two.wait_recv()
+        far_half(0)
+        tail_far[1].wait_recv()
+
+    @pl.when(odd)
+    def _():
+        far[1].wait_recv()
+        twin_far[1].wait_recv()
+
+    far_half(1)
     keep(PAIR, f_pair)
-
-    for h in range(2):
-        far[h].wait_recv()
-        on(even, twin_far[h].start)
-    keep(NEXT, f_next)
-    for h in range(2):
-        on(odd, twin_far[h].wait_recv)
-
-        @pl.when(even)
-        def _(h=h):
-            tail_far[h].wait_recv()
-            if h == GO_AT:
-                pl.semaphore_signal(go, inc=1, device_id=twin, device_id_type=MESH)
-
-        split(FAR, h * HALF, HALF)
-    make(1, PAIR, FAR, f_far, pair).start()
-
-    @pl.when(odd)
-    def _():
-        pl.semaphore_wait(go, 1)
-        for copy in near:
-            copy.start()
-
     keep(FAR, f_far)
 
     for copy in along + far + across + [tail_along]:
         copy.wait_send()
     on(has_next, tail_out.wait_send, label_out.wait_send, relay[0].wait_send, relay[1].wait_send)
-    on(even, *(c.wait_send for c in [*tail_far, *twin_pair, *twin_far, twin_own, label_twin]))
+    on(even, *(c.wait_send for c in [*tail_far, round_one, round_two, *twin_pair, *twin_far, twin_own, label_twin]))
     for copy in gifts:
         copy.wait()
     assert len(names) <= SEMAPHORES
 
 
 SEMAPHORES = 32
-GO_AT = 0
+AROUND = 128
 
 
 def shards(intensity, cycle_label):
@@ -280,6 +307,7 @@
         scratch_shapes=[
             pltpu.VMEM((4, ROWS, COLS), jnp.float32),
             pltpu.VMEM((4, ROWS, TAIL), jnp.float32),
+            pltpu.VMEM((AROUND, TAIL), jnp.float32),
             pltpu.VMEM((1, COLS), jnp.int32),
             pltpu.VMEM((1, TAIL), jnp.int32),
             pltpu.VMEM((4, ROWS, DEPTH), jnp.bfloat16),

time: 103 us -> 100 us (0.971); the launches traced: 103 us -> 98.5 us
  Pallas kernels: 99.2 us -> 95.1 us
    pallas_call x1, Pallas kernels: 99.2 us -> 95.1 us  [shards(): pl.pallas_call(kernel, out_shape=pltpu.VMEM((1, ROWS, 8 * ROWS), jnp.floa...]
where the time goes in v4:
time: 100 us; the launch traced here: 98.5 us
  Pallas kernels  95.1 us (95%)
  local copies, waits for them, and re-layouts  3.4 us (3%)
    pallas_call x1, Pallas kernels, shards(): pl.pallas_call(kernel, out_shape=pltpu.VMEM((1, ROWS, 8 * ROWS), jnp.floa...  95.1 us
    unnamed x1, local copies, waits for them, and re-layouts  3.4 us

profile of v4, /device:TPU:7, one launch (start us, length us, event | category | flops | bytes accessed | tf_op | source)
XLA Modules:
  0.0 98.5 jit_solution(453139385435491852)
XLA Ops:
  0.0 95.1 %gram_maps.1 = f32[1,512,4096]{2,1,0:T(8,128)S(1)} custom-call(f32[512,1024]{1,0:T(8,128)} %x_ref.1, s32[1,1024]{1,0:T(1,128)} %bitcast.1), custom_call_target="tpu_custom_call" | custom-call | tf_op jit(solution)/shard_map/gram_maps/pallas_call | solution.py:302
  95.1 3.4 %copy.4 = f32[1,512,4096]{2,1,0:T(8,128)} copy(f32[1,512,4096]{2,1,0:T(8,128)S(1)} %gram_maps.1) | data formatting | bytes 16777216

commit v5 on v4

--- a/solution.py
+++ b/solution.py
@@ -20,7 +20,7 @@
 
 def kernel(
     x_ref, label_hbm, out_ref,
-    xm, xt, passing, label_ref, tail_label, hi, lo, row_scale, col_scale, inverse, block,
+    xm, xt, passing, label_ref, tail_label, hi, lo, row_scale, col_scale, inverse, block, lifted, carried,
     send, recv, local, go,
 ):
     f = lax.axis_index("frame")
@@ -31,11 +31,13 @@
     f_last = a * 4 + (b + 3 - turn) % 4
     f_far = a * 4 + (b + 2) % 4
     f_pair = (1 - a) * 4 + b
+    f_carried = (1 - a) * 4 + (b + 3) % 4
     even = r % 2 == 0
     odd = r % 2 == 1
     has_next = jnp.logical_and(odd, r < 15)
     has_prev = jnp.logical_and(even, r > 0)
     nxt, last, pair = (f_next, r), (f_last, r), (f_pair, r)
+    above = (a * 4 + (b + 1) % 4, r)
     twin = (f, r + 1 - turn)
     following = (f_pair, r + 1)
     preceding = (f_pair, r - 1)
@@ -241,22 +243,33 @@
     make(0, PAIR, NEXT, f_next, pair, HALF, HALF).start()
 
     far_gift = [None, None]
+    below = pl.ds(LIFT, ROWS - LIFT)
 
     def far_half(h):
         split(FAR, h * HALF, HALF)
-        product(PAIR, FAR, block.at[1], 0, 0, ROWS, h * HALF, HALF)
+        product(PAIR, FAR, block.at[1], 0, LIFT, ROWS - LIFT, h * HALF, HALF)
         far_gift[h].start()
 
     for h in range(2):
-        dst = out_ref.at[0, :, pl.ds(pl.multiple_of(f_far * ROWS + h * HALF, TILE), HALF)]
-        far_gift[h] = remote(f"far_gift{h}", block.at[1, :, pl.ds(h * HALF, HALF)], dst, pair)
+        dst = out_ref.at[0, below, pl.ds(pl.multiple_of(f_far * ROWS + h * HALF, TILE), HALF)]
+        far_gift[h] = remote(f"far_gift{h}", block.at[1, below, pl.ds(h * HALF, HALF)], dst, pair)
     gifts.extend(far_gift)
+
+    lift = remote("lift", lifted, carried, above)
+    dst = out_ref.at[0, pl.ds(0, LIFT), pl.ds(pl.multiple_of(f_carried * ROWS, ROWS), ROWS)]
+    carry = remote("carry", carried, dst, above)
+    gifts.append(carry)
+
+    def start_lift():
+        product(FAR, PAIR, lifted, 0, 0, LIFT)
+        lift.start()
 
     @pl.when(odd)
     def _():
         far[0].wait_recv()
         twin_far[0].wait_recv()
         far_half(0)
+        start_lift()
         pl.semaphore_wait(go, 1)
 
     @pl.when(even)
@@ -267,13 +280,17 @@
         pl.semaphore_signal(go, inc=1, device_id=twin, device_id_type=MESH)
 
     near.start()
-    make(3, NEXT, PAIR, f_pair, nxt).start()
 
     @pl.when(even)
     def _():
         round_two.wait_recv()
         far_half(0)
-        tail_far[1].wait_recv()
+        start_lift()
+
+    make(3, NEXT, PAIR, f_pair, nxt, col=0, cols=HALF).start()
+    second = make(3, NEXT, PAIR, f_pair, nxt, col=HALF, cols=HALF)
+    on(odd, second.start)
+    on(even, tail_far[1].wait_recv)
 
     @pl.when(odd)
     def _():
@@ -282,9 +299,12 @@
 
     far_half(1)
     keep(PAIR, f_pair)
+    lift.wait_recv()
+    carry.start()
+    on(even, second.start)
     keep(FAR, f_far)
 
-    for copy in along + far + across + [tail_along]:
+    for copy in along + far + across + [tail_along, lift]:
         copy.wait_send()
     on(has_next, tail_out.wait_send, label_out.wait_send, relay[0].wait_send, relay[1].wait_send)
     on(even, *(c.wait_send for c in [*tail_far, round_one, round_two, *twin_pair, *twin_far, twin_own, label_twin]))
@@ -294,7 +314,8 @@
 
 
 SEMAPHORES = 32
-AROUND = 128
+AROUND = 96
+LIFT = 32
 
 
 def shards(intensity, cycle_label):
@@ -316,6 +337,8 @@
             pltpu.VMEM((4, 8, ROWS), jnp.float32),
             pltpu.VMEM((ROWS, 128), jnp.float32),
             pltpu.VMEM((4, ROWS, ROWS), jnp.float32),
+            pltpu.VMEM((LIFT, ROWS), jnp.float32),
+            pltpu.VMEM((LIFT, ROWS), jnp.float32),
             pltpu.SemaphoreType.DMA((SEMAPHORES,)),
             pltpu.SemaphoreType.DMA((SEMAPHORES,)),
             pltpu.SemaphoreType.DMA((2,)),

time: 100 us -> 99 us (0.990); the launches traced: 98.5 us -> 98.9 us
  no operation moved by 1% of the time
where the time goes in v5:
time: 99 us; the launch traced here: 98.9 us
  Pallas kernels  95.5 us (96%)
  local copies, waits for them, and re-layouts  3.4 us (3%)
    pallas_call x1, Pallas kernels, shards(): pl.pallas_call(kernel, out_shape=pltpu.VMEM((1, ROWS, 8 * ROWS), jnp.floa...  95.5 us
    unnamed x1, local copies, waits for them, and re-layouts  3.4 us

profile of v5, /device:TPU:7, one launch (start us, length us, event | category | flops | bytes accessed | tf_op | source)
XLA Modules:
  0.0 98.9 jit_solution(10966132827096142370)
XLA Ops:
  0.0 95.5 %gram_maps.1 = f32[1,512,4096]{2,1,0:T(8,128)S(1)} custom-call(f32[512,1024]{1,0:T(8,128)} %x_ref.1, s32[1,1024]{1,0:T(1,128)} %bitcast.1), custom_call_target="tpu_custom_call" | custom-call | tf_op jit(solution)/shard_map/gram_maps/pallas_call | solution.py:323
  95.5 3.4 %copy.4 = f32[1,512,4096]{2,1,0:T(8,128)} copy(f32[1,512,4096]{2,1,0:T(8,128)S(1)} %gram_maps.1) | data formatting | bytes 16777216

commit v6 on v5

--- a/solution.py
+++ b/solution.py
@@ -242,23 +242,23 @@
     split(PAIR, HALF, HALF)
     make(0, PAIR, NEXT, f_next, pair, HALF, HALF).start()
 
-    far_gift = [None, None]
     below = pl.ds(LIFT, ROWS - LIFT)
 
-    def far_half(h):
+    def far_copy(h, up):
+        dst = out_ref.at[0, up, pl.ds(pl.multiple_of(f_far * ROWS + h * HALF, TILE), HALF)]
+        return remote(f"far_gift{h}", block.at[1, up, pl.ds(h * HALF, HALF)], dst, pair)
+
+    whole = [far_copy(h, pl.ds(0, ROWS)) for h in range(2)]
+    short = [far_copy(h, below) for h in range(2)]
+
+    def far_half(h, start, copies):
         split(FAR, h * HALF, HALF)
-        product(PAIR, FAR, block.at[1], 0, LIFT, ROWS - LIFT, h * HALF, HALF)
-        far_gift[h].start()
-
-    for h in range(2):
-        dst = out_ref.at[0, below, pl.ds(pl.multiple_of(f_far * ROWS + h * HALF, TILE), HALF)]
-        far_gift[h] = remote(f"far_gift{h}", block.at[1, below, pl.ds(h * HALF, HALF)], dst, pair)
-    gifts.extend(far_gift)
+        product(PAIR, FAR, block.at[1], 0, start, ROWS - start, h * HALF, HALF)
+        copies[h].start()
 
     lift = remote("lift", lifted, carried, above)
     dst = out_ref.at[0, pl.ds(0, LIFT), pl.ds(pl.multiple_of(f_carried * ROWS, ROWS), ROWS)]
     carry = remote("carry", carried, dst, above)
-    gifts.append(carry)
 
     def start_lift():
         product(FAR, PAIR, lifted, 0, 0, LIFT)
@@ -268,7 +268,7 @@
     def _():
         far[0].wait_recv()
         twin_far[0].wait_recv()
-        far_half(0)
+        far_half(0, LIFT, short)
         start_lift()
         pl.semaphore_wait(go, 1)
 
@@ -284,30 +284,34 @@
     @pl.when(even)
     def _():
         round_two.wait_recv()
-        far_half(0)
-        start_lift()
+        far_half(0, 0, whole)
 
     make(3, NEXT, PAIR, f_pair, nxt, col=0, cols=HALF).start()
     second = make(3, NEXT, PAIR, f_pair, nxt, col=HALF, cols=HALF)
-    on(odd, second.start)
-    on(even, tail_far[1].wait_recv)
+    second.start()
+
+    @pl.when(even)
+    def _():
+        tail_far[1].wait_recv()
+        far_half(1, 0, whole)
 
     @pl.when(odd)
     def _():
         far[1].wait_recv()
         twin_far[1].wait_recv()
-
-    far_half(1)
+        far_half(1, LIFT, short)
+        lift.wait_recv()
+        carry.start()
+
     keep(PAIR, f_pair)
-    lift.wait_recv()
-    carry.start()
-    on(even, second.start)
     keep(FAR, f_far)
 
-    for copy in along + far + across + [tail_along, lift]:
+    for copy in along + far + across + [tail_along]:
         copy.wait_send()
     on(has_next, tail_out.wait_send, label_out.wait_send, relay[0].wait_send, relay[1].wait_send)
     on(even, *(c.wait_send for c in [*tail_far, round_one, round_two, *twin_pair, *twin_far, twin_own, label_twin]))
+    on(odd, lift.wait_send, carry.wait, *(c.wait for c in short))
+    on(even, *(c.wait for c in whole))
     for copy in gifts:
         copy.wait()
     assert len(names) <= SEMAPHORES
@@ -315,7 +319,7 @@
 
 SEMAPHORES = 32
 AROUND = 96
-LIFT = 32
+LIFT = 64
 
 
 def shards(intensity, cycle_label):

time: 99 us -> 99 us (level)
  no operation moved by 1% of the time
where the time goes in v6:
time: 99 us; the launch traced here: 98.9 us
  Pallas kernels  95.5 us (96%)
  local copies, waits for them, and re-layouts  3.4 us (3%)
    pallas_call x1, Pallas kernels, shards(): pl.pallas_call(kernel, out_shape=pltpu.VMEM((1, ROWS, 8 * ROWS), jnp.floa...  95.5 us
    unnamed x1, local copies, waits for them, and re-layouts  3.4 us

profile of v6, /device:TPU:7, one launch (start us, length us, event | category | flops | bytes accessed | tf_op | source)
XLA Modules:
  0.0 98.9 jit_solution(16343606686492288672)
XLA Ops:
  0.0 95.5 %gram_maps.1 = f32[1,512,4096]{2,1,0:T(8,128)S(1)} custom-call(f32[512,1024]{1,0:T(8,128)} %x_ref.1, s32[1,1024]{1,0:T(1,128)} %bitcast.1), custom_call_target="tpu_custom_call" | custom-call | tf_op jit(solution)/shard_map/gram_maps/pallas_call | solution.py:327
  95.5 3.4 %copy.4 = f32[1,512,4096]{2,1,0:T(8,128)} copy(f32[1,512,4096]{2,1,0:T(8,128)S(1)} %gram_maps.1) | data formatting | bytes 16777216

commit v7 on v6

--- a/solution.py
+++ b/solution.py
@@ -318,7 +318,7 @@
 
 
 SEMAPHORES = 32
-AROUND = 96
+AROUND = 112
 LIFT = 64
 
 

time: 99 us -> 99 us (level)
  no operation moved by 1% of the time
where the time goes in v7:
time: 99 us; the launch traced here: 98.8 us
  Pallas kernels  95.4 us (96%)
  local copies, waits for them, and re-layouts  3.4 us (3%)
    pallas_call x1, Pallas kernels, shards(): pl.pallas_call(kernel, out_shape=pltpu.VMEM((1, ROWS, 8 * ROWS), jnp.floa...  95.4 us
    unnamed x1, local copies, waits for them, and re-layouts  3.4 us

profile of v7, /device:TPU:7, one launch (start us, length us, event | category | flops | bytes accessed | tf_op | source)
XLA Modules:
  0.0 98.8 jit_solution(17169293148207624415)
XLA Ops:
  0.0 95.4 %gram_maps.1 = f32[1,512,4096]{2,1,0:T(8,128)S(1)} custom-call(f32[512,1024]{1,0:T(8,128)} %x_ref.1, s32[1,1024]{1,0:T(1,128)} %bitcast.1), custom_call_target="tpu_custom_call" | custom-call | tf_op jit(solution)/shard_map/gram_maps/pallas_call | solution.py:327
  95.4 3.4 %copy.4 = f32[1,512,4096]{2,1,0:T(8,128)} copy(f32[1,512,4096]{2,1,0:T(8,128)S(1)} %gram_maps.1) | data formatting | bytes 16777216
